TPU v7x, 256 devices: a whole 4x4x8 slice. The times are simulated.
256 devices in a mesh: rows: 16 (over z, x_lo), cols: 16 (over x_hi, y, core).
Axes of the slice: x: 4 (x_hi: 2, x_lo: 2; x = x_hi * 2 + x_lo), y: 4, z: 8, core: 2. Of those that a mesh axis runs over, the one named last changes fastest.
Arguments:
- columns: bfloat16 [16384, 8192], P('rows', 'cols'), may hold values from -30 to 30
- column_order: int32 [512], replicated, may hold values from 0 to 511, each once
- section_bits: int32 [3], replicated, may hold values from 0 to 3, as said below
Outputs:
- rotated: float32 [16384, 8192], P('rows', 'cols')
Inputs may be any that keep to these rules, and one draw needn't show every extreme that they name: `section_bits`: bit numbers of a column pair index, repeats allowed; bit 0 and the highest bit are always among them.
All inputs are finite; a program needn't handle non-finite values.
Results may differ from a plain program's by a relative error of at most 0.0046.
Values may be sent and summed in bfloat16 or wider, within the bound.
A program may use at most 64 MiB of HBM per device.

v0:
```python
from functools import partial

import jax
import jax.numpy as jnp
from jax import lax
from jax.sharding import PartitionSpec as P

SECTIONS = 3
ITERS = 4


EPS = 1e-06
THETA = 4.0
HIGH = lax.Precision.HIGHEST


def shortened(shard):

    def short(part):
        return part.astype(jnp.bfloat16) if part.dtype == jnp.float32 else part

    return jax.tree.map(short, shard)


def swapped(block, axis, distance):
    count = lax.axis_size(axis)
    route = []
    for low in range(count):
        high = low | 1 << distance
        if high != low and high < count:
            route += [(low, high), (high, low)]
    return lax.ppermute(block, axis, route)


def whole_rotation(gram_matrix):
    pair_width = gram_matrix.shape[0]
    ramp_values = jnp.arange(pair_width, dtype=jnp.float32) / pair_width
    root_values = jnp.sqrt(jnp.diagonal(gram_matrix) + EPS)
    scaled_gram = gram_matrix / (root_values[:, None] * root_values[None, :])
    commutator = THETA * (ramp_values[:, None] - ramp_values[None, :]) * scaled_gram
    frobenius = jnp.sum(commutator * commutator)
    iterate = (jnp.eye(pair_width, dtype=jnp.float32) + commutator) / jnp.sqrt(1.0 + frobenius)
    for sweep_index in range(ITERS):
        product = lax.dot_general(
            iterate,
            iterate,
            (((0,), (0,)), ((), ())),
            precision=HIGH,
            preferred_element_type=jnp.float32,
        )
        iterate = 1.5 * iterate - 0.5 * jnp.dot(
            iterate, product, precision=HIGH, preferred_element_type=jnp.float32
        )
    return iterate


def partner_block(moving, bit_level):
    return jax.tree.map(
        lambda part, own: part.astype(own.dtype),
        swapped(shortened(moving), "cols", bit_level),
        moving,
    )


def shards(columns, column_order, section_bits):
    half_width = columns.shape[1] // 2
    column_pair = jnp.take(columns, column_order, axis=1)
    level_count = lax.axis_size("cols").bit_length() - 1
    branches = [partial(partner_block, bit_level=bit_level) for bit_level in range(level_count)]
    result = None
    for section_index in range(SECTIONS):
        incoming = lax.switch(section_bits[section_index], branches, column_pair[:, half_width:])
        column_pair = jnp.concatenate([column_pair[:, :half_width], incoming], axis=1)
        local_gram = lax.dot_general(
            column_pair, column_pair, (((0,), (0,)), ((), ())), preferred_element_type=jnp.float32
        )
        gram_matrix = lax.psum(local_gram, "rows")
        rotation_matrix = whole_rotation(gram_matrix)
        turned = jnp.dot(
            column_pair.astype(jnp.float32),
            rotation_matrix,
            precision=HIGH,
            preferred_element_type=jnp.float32,
        )
        if section_index + 1 < SECTIONS:
            column_pair = turned.astype(jnp.bfloat16)
        else:
            result = turned
    return result


def solution(mesh):
    return jax.shard_map(
        shards,
        mesh=mesh,
        in_specs=(P("rows", "cols"), P(), P()),
        out_specs=P("rows", "cols"),
        check_vma=False,
    )
```

profile of v0, /device:TPU:8, one launch (start us, length us, event | category | flops | bytes accessed | tf_op | source)
XLA Modules:
  0.0 560.7 jit_solution(6680550959656041310)
XLA Ops:
  9.4 2.1 gather_fusion
  13.4 2.5 conditional.3
  13.8 1.9 collective-permute-done
  18.4 141.6 %all-reduce.4.cloned.1.call-done = f32[512,512]{1,0:T(8,128)} async-done(((f32[512,512]{1,0:T(8,128)}), f32[512,512]{1,0:T(8,128)}) %all-reduce.4.cloned.1.call-update) | async-done | bytes 1048592 | tf_op jit(solution)/shard_map/psum | solution.py:77
  159.9 9.1 %gather_fusion.1 = f32[512]{0:T(512)S(1)} fusion(f32[512,512]{1,0:T(8,128)} %all-reduce.4.cloned.1.call-done, s32[512]{0:T(512)S(1)} %bitcast.48), kind=kCustom, calls=%fused_computation.1 | custom fusion | bytes 8192 | tf_op jit(solution)/shard_map/jit(diagonal)/cond/branch_0_fun/gather | solution.py:38
  170.9 2.6 fusion.25
  173.5 2.3 fusion.11
  179.6 1.9 fusion.36
  181.5 2.1 fusion.9
  183.6 1.9 fusion.37
  189.3 11.3 %conditional.4 = (bf16[1024,256]{0,1:T(8,128)(2,1)S(1)}) conditional(s32[]{:T(128)} %bitcast.3, (bf16[1024,512]{0,1:T(8,128)(2,1)S(1)}) %tuple.50, (bf16[1024,512]{0,1:T(8,128)(2,1)S(1)}) %tuple.50, (bf16[1024,512]{0,1:T(8,128)(2,1)S(1)}) %tuple.50, (bf16[1024,512]{0,1:T(8,128)(2,1)S(1)}) %tuple.50), branch_computations={%region_6.7_spmd, %region_7.8_spmd, %region_8.9_spmd, %region_9.10... | conditional | bytes 5242928 | solution.py:72
  189.6 2.2 collective-permute-start.6
  191.8 8.6 %collective-permute-done.6 = bf16[1024,256]{1,0:T(8,128)(2,1)S(1)} collective-permute-done((bf16[1024,256]{1,0:T(8,128)(2,1)S(1)}, bf16[1024,256]{1,0:T(8,128)(2,1)S(1)}, u32[]{:S(2)}, u32[]{:S(2)}) %collective-permute-start.6) | collective-permute-done | bytes 524320 | tf_op jit(solution)/shard_map/cond/branch_2_fun/ppermute | solution.py:32
  203.1 138.6 %all-reduce.6.cloned.1.call-done = f32[512,512]{1,0:T(8,128)} async-done(((f32[512,512]{1,0:T(8,128)}), f32[512,512]{1,0:T(8,128)}) %all-reduce.6.cloned.1.call-update) | async-done | bytes 1048592 | tf_op jit(solution)/shard_map/psum | solution.py:77
  341.7 8.9 %gather_fusion.2 = f32[512]{0:T(512)S(1)} fusion(f32[512,512]{1,0:T(8,128)} %all-reduce.6.cloned.1.call-done, s32[512]{0:T(512)S(1)} %bitcast.49), kind=kCustom, calls=%fused_computation.2 | custom fusion | bytes 8192 | tf_op jit(solution)/shard_map/jit(diagonal)/cond/branch_0_fun/gather | solution.py:38
  352.4 2.6 fusion.22
  355.1 2.3 fusion.7
  361.1 1.9 fusion.39
  363.1 2.3 fusion.5
  365.4 1.9 fusion.40
  371.1 11.3 %conditional.5 = (bf16[1024,256]{0,1:T(8,128)(2,1)S(1)}) conditional(s32[]{:T(128)} %bitcast.4, (bf16[1024,512]{0,1:T(8,128)(2,1)S(1)}) %tuple.55, (bf16[1024,512]{0,1:T(8,128)(2,1)S(1)}) %tuple.55, (bf16[1024,512]{0,1:T(8,128)(2,1)S(1)}) %tuple.55, (bf16[1024,512]{0,1:T(8,128)(2,1)S(1)}) %tuple.55), branch_computations={%region_12.13_spmd, %region_13.14_spmd, %region_14.15_spmd, %regio... | conditional | bytes 5242928 | solution.py:72
  371.4 3.1 collective-permute-start.11
  374.5 7.7 %collective-permute-done.11 = bf16[1024,256]{1,0:T(8,128)(2,1)S(1)} collective-permute-done((bf16[1024,256]{1,0:T(8,128)(2,1)S(1)}, bf16[1024,256]{1,0:T(8,128)(2,1)S(1)}, u32[]{:S(2)}, u32[]{:S(2)}) %collective-permute-start.11) | collective-permute-done | bytes 524320 | tf_op jit(solution)/shard_map/cond/branch_3_fun/ppermute | solution.py:32
  384.1 139.4 %all-reduce.8.cloned.1.call-done = f32[512,512]{1,0:T(8,128)} async-done(((f32[512,512]{1,0:T(8,128)}), f32[512,512]{1,0:T(8,128)}) %all-reduce.8.cloned.1.call-update) | async-done | bytes 1048592 | tf_op jit(solution)/shard_map/psum | solution.py:77
  523.5 8.8 %gather_fusion.3 = f32[512]{0:T(512)S(1)} fusion(f32[512,512]{1,0:T(8,128)} %all-reduce.8.cloned.1.call-done, s32[512]{0:T(512)S(1)} %bitcast.50), kind=kCustom, calls=%fused_computation.3 | custom fusion | bytes 8192 | tf_op jit(solution)/shard_map/jit(diagonal)/cond/branch_0_fun/gather | solution.py:38
  534.2 2.6 fusion.19
  536.8 2.3 fusion.3
  541.0 1.9 fusion.2
  542.9 1.9 fusion.42
  544.8 2.1 fusion.1
  546.9 1.9 fusion.43
  550.7 3.2 fusion.15
  (54 shorter events, 33.0 us)
Async XLA Ops:
  6.5 153.4 %all-reduce.4.cloned.1.call-start = ((), (), s32[]{:S(2)}) async-start(), calls=%async_computation | async-start | bytes 2097152 | tf_op jit(solution)/shard_map/psum | solution.py:77
  11.5 0.7 copy-start.3
  13.7 2.0 collective-permute-start
  17.7 324.0 %all-reduce.6.cloned.1.call-start = ((), (), s32[]{:S(2)}) async-start(), calls=%async_computation.1 | async-start | bytes 2097152 | tf_op jit(solution)/shard_map/psum | solution.py:77
  159.9 9.2 %copy-start.1 = (f32[512,512]{1,0:T(8,128)S(1)}, f32[512,512]{1,0:T(8,128)}, u32[]{:S(2)}) copy-start(f32[512,512]{1,0:T(8,128)} %all-reduce.4.cloned.1.call-done) | copy-start | bytes 3145732
  189.6 10.8 %collective-permute-start.6 = (bf16[1024,256]{1,0:T(8,128)(2,1)S(1)}, bf16[1024,256]{1,0:T(8,128)(2,1)S(1)}, u32[]{:S(2)}, u32[]{:S(2)}) collective-permute-start(bf16[1024,256]{1,0:T(8,128)(2,1)S(1)} %copy.28), channel_id=1, source_target_pairs={{0,4},{4,0},{1,5},{5,1},{2,6},{6,2},{3,7},{7,3},{8,12},{12,8},{9,1... | collective-permute-start | bytes 1572872 | tf_op jit(solution)/shard_map/cond/branch_2_fun/ppermute | solution.py:32
  202.4 321.1 %all-reduce.8.cloned.1.call-start = ((), (), s32[]{:S(2)}) async-start(), calls=%async_computation.2 | async-start | bytes 2097152 | tf_op jit(solution)/shard_map/psum | solution.py:77
  341.7 8.9 %copy-start = (f32[512,512]{1,0:T(8,128)S(1)}, f32[512,512]{1,0:T(8,128)}, u32[]{:S(2)}) copy-start(f32[512,512]{1,0:T(8,128)} %all-reduce.6.cloned.1.call-done) | copy-start | bytes 3145732
  371.4 10.8 %collective-permute-start.11 = (bf16[1024,256]{1,0:T(8,128)(2,1)S(1)}, bf16[1024,256]{1,0:T(8,128)(2,1)S(1)}, u32[]{:S(2)}, u32[]{:S(2)}) collective-permute-start(bf16[1024,256]{1,0:T(8,128)(2,1)S(1)} %copy.34), channel_id=1, source_target_pairs={{0,8},{8,0},{1,9},{9,1},{2,10},{10,2},{3,11},{11,3},{4,12},{12,4},... | collective-permute-start | bytes 1572872 | tf_op jit(solution)/shard_map/cond/branch_3_fun/ppermute | solution.py:32
  523.5 8.9 %copy-start.2 = (f32[512,512]{1,0:T(8,128)S(1)}, f32[512,512]{1,0:T(8,128)}, u32[]{:S(2)}) copy-start(f32[512,512]{1,0:T(8,128)} %all-reduce.8.cloned.1.call-done) | copy-start | bytes 3145732
Sparse Core Ops, SparseCore 0:
  17.8 142.0 all-reduce.3
  202.5 139.1 all-reduce.5
  384.2 139.2 all-reduce.7
where the time goes:
time: 567 us; the launch traced here: 561 us
  waiting for transfers between devices  438 us (77%)
  matrix products  61.7 us (11%)
  local copies, waits for them, and re-layouts  33 us (6%)
  between operations  17.7 us (3%)
    psum x3, waiting for transfers between devices, shards(): gram_matrix = lax.psum(local_gram, 'rows')  420 us
    gather x3, local copies, waits for them, and re-layouts, whole_rotation(): root_values = jnp.sqrt(jnp.diagonal(gram_matrix) + EPS)  26.9 us
    dot_general x12, matrix products, whole_rotation(): lax.dot_general(iterate, iterate, (((0,), (0,)), ((), ())), precision=HIG...  24.9 us
    dot_general x12, matrix products, whole_rotation(): jnp.dot(iterate, product, precision=HIGH, preferred_element_type=jnp.floa...  24.7 us
    ppermute x3, waiting for transfers between devices, swapped(): return lax.ppermute(block, axis, route)  18.2 us
  transfers between devices with their start and end apart: 6, of which 6 were waited for; matrix products, arithmetic and copies ran while one was open for 0% of the time, Pallas kernels for 0%

commit v1 on v0

v1 whole, which is shorter than its diff:
```python
import functools

import jax
import jax.numpy as jnp
from jax import lax
from jax.experimental import pallas as pl
from jax.experimental.pallas import tpu as pltpu
from jax.sharding import PartitionSpec as P

SECTIONS = 3
ITERS = 4
EPS = 1e-06
THETA = 4.0
MESH = pl.DeviceIdType.MESH
BF = jnp.bfloat16
F32 = jnp.float32
TILE = 256


def dot(a, b):
    return jnp.dot(a, b, preferred_element_type=F32)


def dot_tn(a, b):
    return lax.dot_general(a, b, (((0,), (0,)), ((), ())), preferred_element_type=F32)


def dot_nt(a, b):
    return lax.dot_general(a, b, (((1,), (1,)), ((), ())), preferred_element_type=F32)


def split(a):
    high = a.astype(BF)
    return high, (a - high.astype(F32)).astype(BF)


def packed(block):
    half = block.shape[0] // 2
    return jnp.concatenate([block[:half, :], block[half:, half:]], axis=1)


def unpacked(block):
    half = block.shape[0]
    a, b, d = block[:, :half], block[:, half : 2 * half], block[:, 2 * half :]
    return jnp.concatenate(
        [jnp.concatenate([a, b], axis=1), jnp.concatenate([b.T, d], axis=1)], axis=0
    )


def rotation(kk, km, mm):
    width = kk.shape[0]
    total = 2 * width
    row = lax.broadcasted_iota(jnp.int32, (width, width), 0)
    col = lax.broadcasted_iota(jnp.int32, (width, width), 1)
    eye = row == col
    gap = (row - col).astype(F32) * (THETA / total)

    def inverse_roots(block, axis):
        d = jnp.sum(jnp.where(eye, block, 0.0), axis=axis, keepdims=True)
        return 1.0 / jnp.sqrt(d + EPS)

    k_col, k_row = inverse_roots(kk, 1), inverse_roots(kk, 0)
    m_col, m_row = inverse_roots(mm, 1), inverse_roots(mm, 0)
    c_kk = gap * (kk * (k_col * k_row))
    c_mm = gap * (mm * (m_col * m_row))
    c_km = (gap - THETA * 0.5) * (km * (k_col * m_row))
    frob = jnp.sum(c_kk * c_kk) + 2.0 * jnp.sum(c_km * c_km) + jnp.sum(c_mm * c_mm)
    z = jnp.concatenate(
        [jnp.concatenate([c_kk, c_km], axis=1), jnp.concatenate([-c_km.T, c_mm], axis=1)],
        axis=0,
    )
    scale = 1.0 / jnp.sqrt(jnp.full((1, 1), 1.0, F32) + frob)
    for k in range(ITERS):
        zb = z.astype(BF)
        w = dot_nt(zb, zb)
        if k:
            w = w + (z + z.T)
        square = scale * scale
        b = 1.5 - 0.5 * square
        z = z - (0.5 * square / b) * (w + dot(zb, w.astype(BF)))
        scale = scale * b
    row = lax.broadcasted_iota(jnp.int32, (total, total), 0)
    col = lax.broadcasted_iota(jnp.int32, (total, total), 1)
    return scale * (z + jnp.where(row == col, 1.0, 0.0))


def meet_kernel(bit, kind, p_ref, high_ref, *rest):
    low_ref, rest = (rest[0], rest[1:]) if kind == BF else (None, rest)
    new_ref, pair_ref, gram_a, gram_b, part_a, landed_a, handed, part_b, landed_b, g_ref, swap_sems, sums, hands = rest
    group = lax.axis_size("rows")
    ring = group // 2
    me_r, me_c = lax.axis_index("rows"), lax.axis_index("cols")
    me_z, me_x = me_r // 2, me_r % 2
    rows, total = p_ref.shape
    half = total // 2
    quarter = half // 2
    tiles = rows // TILE
    rows_each = quarter // group
    partner = me_c + (1 << bit) * (1 - 2 * ((me_c // (1 << bit)) % 2))
    sems_a, sems_b = sums.at[0], sums.at[1]
    kk_ref, km_ref, mm_ref = g_ref.at[0], g_ref.at[1], g_ref.at[2]

    def each_peer(act):
        def visit(i, carry):
            k = i // 2
            z = ring // 2 + ((k + 1) // 2) * (1 - 2 * (k % 2))
            act(((me_z + z) % ring) * 2 + (me_x + 1 + i) % 2)
            return carry

        lax.fori_loop(0, group - 1, visit, 0)

    def to(device, source, target, send_sem, recv_sem):
        return pltpu.make_async_remote_copy(
            src_ref=source,
            dst_ref=target,
            send_sem=send_sem,
            recv_sem=recv_sem,
            device_id=device,
            device_id_type=MESH,
        )

    def rows_of(t):
        return pl.ds(pl.multiple_of(t * TILE, TILE), TILE)

    def swap(t):
        return to(
            (me_r, partner),
            new_ref.at[rows_of(t), :],
            pair_ref.at[rows_of(t), half:],
            swap_sems.at[0, t],
            swap_sems.at[1, t],
        )

    def wait_all(buffer, sem):
        others = buffer.at[pl.ds(0, group - 1)]
        pltpu.make_async_copy(others, others, sem).wait()

    def start_sum(part, landed, sems):
        each_peer(
            lambda peer: to(
                (peer, me_c), part.at[peer], landed.at[me_r], sems.at[0], sems.at[1]
            ).start()
        )
        landed[me_r] = part[me_r]

    def end_sum(landed, sems):
        wait_all(landed, sems.at[1])
        out = landed[0].astype(F32)
        for k in range(1, group):
            out += landed[k].astype(F32)
        return out

    def start_gather(gram, sems):
        each_peer(
            lambda peer: to(
                (peer, me_c), gram.at[me_r], gram.at[me_r], sems.at[2], sems.at[3]
            ).start()
        )

    barrier = pltpu.get_barrier_semaphore()
    each_peer(
        lambda peer: pl.semaphore_signal(
            barrier, inc=1, device_id=(peer, me_c), device_id_type=MESH
        )
    )
    pl.semaphore_signal(barrier, inc=1, device_id=(me_r, partner), device_id_type=MESH)

    g_ref[...] = jnp.zeros_like(g_ref)

    def turn_kept(t, carry):
        old = p_ref[rows_of(t), :]
        new = dot(old, high_ref[...])
        if low_ref is not None:
            new += dot(old, low_ref[...])
        new = new.astype(BF)
        pair_ref[rows_of(t), :half] = new
        kk_ref[...] += dot_tn(new, new)
        return carry

    lax.fori_loop(0, tiles, turn_kept, 0)
    pl.semaphore_wait(barrier, group)

    def leave(t, carry):
        swap(t).start()
        return carry

    lax.fori_loop(0, tiles, leave, 0)

    def square(t, carry):
        old = new_ref[rows_of(t), :]
        mm_ref[...] += dot_tn(old, old)
        return carry

    lax.fori_loop(0, tiles, square, 0)
    shape = (group, rows_each, half + quarter)
    part_a[...] = jnp.concatenate(
        [packed(kk_ref[...]).reshape(shape), packed(mm_ref[...]).reshape(shape)], axis=1
    ).astype(kind)
    start_sum(part_a, landed_a, sems_a)

    def cross(t, carry):
        swap(t).wait()
        km_ref[...] += dot_tn(pair_ref[rows_of(t), :half], pair_ref[rows_of(t), half:])
        return carry

    lax.fori_loop(0, tiles - 1, cross, 0)
    if bit == 0:
        lax.fori_loop(tiles - 1, tiles, cross, 0)
        part_b[...] = km_ref[...].reshape(group, half // group, half).astype(kind)
        start_sum(part_b, landed_b, sems_b)
    mine = end_sum(landed_a, sems_a)
    gram_a[me_r] = mine.astype(kind)
    hand = to((me_r, partner), gram_a.at[me_r], handed, hands.at[0], hands.at[1])
    hand.start()
    if bit:
        lax.fori_loop(tiles - 1, tiles, cross, 0)
        part_b[...] = km_ref[...].reshape(group, half // group, half).astype(kind)
        start_sum(part_b, landed_b, sems_b)
    hand.wait()
    place = lax.broadcasted_iota(jnp.int32, mine.shape, 0)
    gram_a[me_r] = jnp.where(place < rows_each, mine, handed[...].astype(F32)).astype(kind)
    start_gather(gram_a, sems_a)
    gram_b[me_r] = end_sum(landed_b, sems_b).astype(kind)
    start_gather(gram_b, sems_b)
    wait_all(part_a, sems_a.at[0])
    wait_all(part_b, sems_b.at[0])
    wait_all(gram_a, sems_a.at[3])
    wait_all(gram_b, sems_b.at[3])
    wait_all(gram_a, sems_a.at[2])
    wait_all(gram_b, sems_b.at[2])


def meet(p, *rest, bit, kind, site):
    rows, total = p.shape
    half, quarter = total // 2, total // 4
    group = lax.axis_size("rows")
    chunk = half // group
    side = (group, chunk, half + quarter)
    full = (group, chunk, half)
    vmem = pl.BlockSpec(memory_space=pltpu.VMEM)
    return pl.pallas_call(
        functools.partial(meet_kernel, bit, kind),
        out_shape=(
            jax.ShapeDtypeStruct((rows, total), BF),
            jax.ShapeDtypeStruct(side, kind),
            jax.ShapeDtypeStruct(full, kind),
        ),
        in_specs=[vmem] * (1 + len(rest)),
        out_specs=[vmem] * 3,
        scratch_shapes=[
            pltpu.VMEM(side, kind),
            pltpu.VMEM(side, kind),
            pltpu.VMEM(side[1:], kind),
            pltpu.VMEM(full, kind),
            pltpu.VMEM(full, kind),
            pltpu.VMEM((3, half, half), F32),
            pltpu.SemaphoreType.DMA((2, rows // TILE)),
            pltpu.SemaphoreType.DMA((2, 4)),
            pltpu.SemaphoreType.DMA((2,)),
        ],
        compiler_params=pltpu.CompilerParams(
            collective_id=site, has_side_effects=True, vmem_limit_bytes=48 << 20
        ),
        name=f"meet_bit{bit}",
    )(p, *rest)


def start_kernel(p_ref, order_ref, high_ref, new_ref):
    rows, total = p_ref.shape
    half = total // 2
    old = lax.broadcasted_iota(jnp.int32, (total, total), 0)
    pick = jnp.where(old == order_ref[...], 1.0, 0.0).astype(BF)
    high_ref[...] = pick[:, :half]
    for t in range(0, rows, TILE):
        new_ref[t : t + TILE, :] = dot(p_ref[t : t + TILE, :], pick[:, half:]).astype(BF)


def start(p, order):
    rows, total = p.shape
    half = total // 2
    return pl.pallas_call(
        start_kernel,
        out_shape=(
            jax.ShapeDtypeStruct((total, half), BF),
            jax.ShapeDtypeStruct((rows, half), BF),
        ),
        compiler_params=pltpu.CompilerParams(vmem_limit_bytes=48 << 20),
        name="start",
    )(p, order)


def turn_kernel(last, p_ref, gram_a, gram_b, *outs):
    rows, total = p_ref.shape
    half = total // 2
    quarter = half // 2
    group = gram_a.shape[0]
    each = quarter // group
    g = gram_a[...].astype(F32)
    kk = unpacked(g[:, :each, :].reshape(quarter, -1))
    mm = unpacked(g[:, each:, :].reshape(quarter, -1))
    high, low = split(rotation(kk, gram_b[...].astype(F32).reshape(half, half), mm))
    if not last:
        high_ref, low_ref, new_ref = outs
        high_ref[...], low_ref[...] = high[:, :half], low[:, :half]
        high, low = high[:, half:], low[:, half:]
    for t in range(0, rows, TILE):
        tile = p_ref[t : t + TILE, :]
        out = dot(tile, high) + dot(tile, low)
        if last:
            outs[0][t : t + TILE, :] = out
        else:
            new_ref[t : t + TILE, :] = out.astype(BF)


def turn(p, gram_a, gram_b, last):
    rows, total = p.shape
    half = total // 2
    out_shape = [jax.ShapeDtypeStruct((rows, total), F32)]
    if not last:
        out_shape = [jax.ShapeDtypeStruct((total, half), BF)] * 2
        out_shape += [jax.ShapeDtypeStruct((rows, half), BF)]
    return pl.pallas_call(
        functools.partial(turn_kernel, last),
        out_shape=out_shape,
        compiler_params=pltpu.CompilerParams(vmem_limit_bytes=48 << 20),
        name="last_turn" if last else "turn",
    )(p, gram_a, gram_b)


def shards(columns, column_order, section_bits):
    levels = lax.axis_size("cols").bit_length() - 1
    p, rest = columns, start(columns, column_order.reshape(1, -1))
    for s in range(SECTIONS):
        branches = [
            functools.partial(meet, bit=bit, kind=BF if s else F32, site=s * levels + bit)
            for bit in range(levels)
        ]
        p, gram_a, gram_b = lax.switch(section_bits[s], branches, p, *rest)
        rest = turn(p, gram_a, gram_b, s + 1 == SECTIONS)
    return rest[0]


def solution(mesh):
    return jax.shard_map(
        shards,
        mesh=mesh,
        in_specs=(P("rows", "cols"), P(), P()),
        out_specs=P("rows", "cols"),
        check_vma=False,
    )
```

time: 567 us -> 121 us (0.21); the launches traced: 561 us -> 121 us
  waiting for transfers between devices: 438 us -> 0 us
  Pallas kernels: 0 us -> 117 us
  matrix products: 61.7 us -> 0 us
  local copies, waits for them, and re-layouts: 33 us -> 2.09 us
  between operations: 17.7 us -> 1.9 us
    psum x3 -> x0, waiting for transfers between devices: 420 us -> none  [shards(): gram_matrix = lax.psum(local_gram, 'rows')]
    pallas_call x0 -> x7, Pallas kernels: none -> 117 us  [the longest x3 102 us: meet(): pl.pallas_call(functools.partial(meet_kernel, bit, kind), out_shape=(jax....]
    dot_general x30 -> x0, matrix products: 61.7 us -> none  [the longest x12 24.9 us: whole_rotation(): lax.dot_general(iterate, iterate, (((0,), (0,)), ((), ())), precision=HIG...]
    gather x4 -> x0, local copies, waits for them, and re-layouts: 28.9 us -> none  [the longest x3 26.9 us: whole_rotation(): root_values = jnp.sqrt(jnp.diagonal(gram_matrix) + EPS)]
    ppermute x3 -> x0, waiting for transfers between devices: 18.2 us -> none  [swapped(): return lax.ppermute(block, axis, route)]
  transfers between devices with their start and end apart: 6 -> 0, of which waited for: 6 -> 0; matrix products, arithmetic and copies ran while one was open for 0% -> 0% of each run, Pallas kernels for 0% -> 0%
where the time goes in v1:
time: 121 us
  Pallas kernels  117 us (97%)
  local copies, waits for them, and re-layouts  2.09 us (2%)
  between operations  1.9 us (2%)
    pallas_call x3, Pallas kernels, meet(): pl.pallas_call(functools.partial(meet_kernel, bit, kind), out_shape=(jax....  102 us
    pallas_call x3, Pallas kernels, turn(): pl.pallas_call(functools.partial(turn_kernel, last), out_shape=out_shape,...  13.2 us

profile of v1, /device:TPU:8, one launch (start us, length us, event | category | flops | bytes accessed | tf_op | source)
XLA Modules:
  0.0 120.9 jit_solution(16087635965775572073)
XLA Ops:
  0.0 1.4 %fusion = (s32[1]{0:T(128)}, s32[1]{0:T(128)}, s32[1]{0:T(128)}) fusion(s32[3]{0:T(128)} %param.17), kind=kLoop, calls=%fused_computation | loop fusion | bytes 24 | tf_op jit(solution)/shard_map/slice | solution.py:338
  3.3 0.0 copy-start
  3.3 0.7 copy-done
  3.9 1.7 %start.1 = (bf16[512,256]{1,0:T(8,128)(2,1)S(1)}, bf16[1024,256]{1,0:T(8,128)(2,1)S(1)}) custom-call(bf16[1024,512]{1,0:T(8,128)(2,1)} %p_ref.1, s32[1,512]{1,0:T(1,128)S(1)} %bitcast.4), custom_call_target="tpu_custom_call" | custom-call | tf_op jit(solution)/shard_map/start/pallas_call | solution.py:281
  5.6 40.3 %conditional.3 = ((bf16[1024,512]{1,0:T(8,128)(2,1)S(1)}, f32[16,16,384]{2,1,0:T(8,128)S(1)}, f32[16,16,256]{2,1,0:T(8,128)S(1)})) conditional(s32[]{:T(128)} %bitcast.2, (bf16[1024,512]{1,0:T(8,128)(2,1)}, bf16[512,256]{1,0:T(8,128)(2,1)S(1)}, bf16[1024,256]{1,0:T(8,128)(2,1)S(1)}) %tuple.41, ...), branch_computations={%region_0.0_spmd, %region_1.0_spmd, %region_2.0_spmd, %region_3.0_... | conditional | bytes 8 | solution.py:338
  5.6 40.3 %meet_bit0.3 = (bf16[1024,512]{1,0:T(8,128)(2,1)S(1)}, f32[16,16,384]{2,1,0:T(8,128)S(1)}, f32[16,16,256]{2,1,0:T(8,128)S(1)}) custom-call(bf16[1024,512]{1,0:T(8,128)(2,1)} %get-tuple-element.93.p_ref, bf16[512,256]{1,0:T(8,128)(2,1)S(1)} %get-tuple-element.94.high_ref, bf16[1024,256]{1,0:T(8,128)(2,1)S(1)} %get-tuple-element.95.rest_0_), custom_call_target="tpu_custom_call" | custom-call | tf_op jit(solution)/shard_map/cond/branch_0_fun/meet_bit0/pallas_call | solution.py:241
  45.9 3.7 %turn.2 = (bf16[512,256]{1,0:T(8,128)(2,1)S(1)}, bf16[512,256]{1,0:T(8,128)(2,1)S(1)}, bf16[1024,256]{1,0:T(8,128)(2,1)S(1)}) custom-call(bf16[1024,512]{1,0:T(8,128)(2,1)S(1)} %get-tuple-element.156.p_ref, f32[16,16,384]{2,1,0:T(8,128)S(1)} %get-tuple-element.157.gram_a, f32[16,16,256]{2,1,0:T(8,128)S(1)} %get-tuple-element.158.gram_b), custom_call_target="tpu_custom_call" | custom-call | tf_op jit(solution)/shard_map/turn/pallas_call | solution.py:322
  49.7 32.4 %conditional.4 = ((bf16[1024,512]{1,0:T(8,128)(2,1)S(1)}, bf16[16,16,384]{2,1,0:T(8,128)(2,1)S(1)}, bf16[16,16,256]{2,1,0:T(8,128)(2,1)S(1)})) conditional(s32[]{:T(128)} %bitcast.1, (bf16[1024,512]{1,0:T(8,128)(2,1)S(1)}, bf16[512,256]{1,0:T(8,128)(2,1)S(1)}, bf16[512,256]{1,0:T(8,128)(2,1)S(1)}, ...), branch_computations={%region_4.0_spmd, %region_5.0_spmd, %region_6.0_spmd, %region_7.0_... | conditional | bytes 8 | solution.py:338
  49.7 32.2 %meet_bit3.4 = (bf16[1024,512]{1,0:T(8,128)(2,1)S(1)}, bf16[16,16,384]{2,1,0:T(8,128)(2,1)S(1)}, bf16[16,16,256]{2,1,0:T(8,128)(2,1)S(1)}) custom-call(bf16[1024,512]{1,0:T(8,128)(2,1)S(1)} %get-tuple-element.117.p_ref, bf16[512,256]{1,0:T(8,128)(2,1)S(1)} %get-tuple-element.118.high_ref, bf16[512,256]{1,0:T(8,128)(2,1)S(1)} %get-tuple-element.119.rest_0_, ...), custom_call_target="tpu_custom_call" | custom-call | tf_op jit(solution)/shard_map/cond/branch_3_fun/meet_bit3/pallas_call | solution.py:241
  82.1 3.8 %turn.3 = (bf16[512,256]{1,0:T(8,128)(2,1)S(1)}, bf16[512,256]{1,0:T(8,128)(2,1)S(1)}, bf16[1024,256]{1,0:T(8,128)(2,1)S(1)}) custom-call(bf16[1024,512]{1,0:T(8,128)(2,1)S(1)} %get-tuple-element.162.p_ref, bf16[16,16,384]{2,1,0:T(8,128)(2,1)S(1)} %get-tuple-element.163.gram_a, bf16[16,16,256]{2,1,0:T(8,128)(2,1)S(1)} %get-tuple-element.164.gram_b), custom_call_target="tpu_custom_call" | custom-call | tf_op jit(solution)/shard_map/turn/pallas_call | solution.py:322
  85.9 29.4 %conditional.5 = ((bf16[1024,512]{1,0:T(8,128)(2,1)S(1)}, bf16[16,16,384]{2,1,0:T(8,128)(2,1)S(1)}, bf16[16,16,256]{2,1,0:T(8,128)(2,1)S(1)})) conditional(s32[]{:T(128)} %bitcast, (bf16[1024,512]{1,0:T(8,128)(2,1)S(1)}, bf16[512,256]{1,0:T(8,128)(2,1)S(1)}, bf16[512,256]{1,0:T(8,128)(2,1)S(1)}, ...), branch_computations={%region_8.0_spmd, %region_9.0_spmd, %region_10.0_spmd, %region_11.... | conditional | bytes 8 | solution.py:338
  85.9 29.3 %meet_bit3.5 = (bf16[1024,512]{1,0:T(8,128)(2,1)S(1)}, bf16[16,16,384]{2,1,0:T(8,128)(2,1)S(1)}, bf16[16,16,256]{2,1,0:T(8,128)(2,1)S(1)}) custom-call(bf16[1024,512]{1,0:T(8,128)(2,1)S(1)} %get-tuple-element.133.p_ref, bf16[512,256]{1,0:T(8,128)(2,1)S(1)} %get-tuple-element.134.high_ref, bf16[512,256]{1,0:T(8,128)(2,1)S(1)} %get-tuple-element.135.rest_0_, ...), custom_call_target="tpu_custom_call" | custom-call | tf_op jit(solution)/shard_map/cond/branch_3_fun/meet_bit3/pallas_call | solution.py:241
  115.3 5.6 %last_turn.1 = f32[1024,512]{1,0:T(8,128)} custom-call(bf16[1024,512]{1,0:T(8,128)(2,1)S(1)} %get-tuple-element.168.p_ref, bf16[16,16,384]{2,1,0:T(8,128)(2,1)S(1)} %get-tuple-element.169.gram_a, bf16[16,16,256]{2,1,0:T(8,128)(2,1)S(1)} %get-tuple-element.170.gram_b), custom_call_target="tpu_custom_call" | custom-call | tf_op jit(solution)/shard_map/last_turn/pallas_call | solution.py:322
Async XLA Ops:
  3.3 0.7 copy-start

commit v2 on v1

--- a/solution.py
+++ b/solution.py
@@ -84,9 +84,16 @@
     return scale * (z + jnp.where(row == col, 1.0, 0.0))
 
 
-def meet_kernel(bit, kind, p_ref, high_ref, *rest):
-    low_ref, rest = (rest[0], rest[1:]) if kind == BF else (None, rest)
-    new_ref, pair_ref, gram_a, gram_b, part_a, landed_a, handed, part_b, landed_b, g_ref, swap_sems, sums, hands = rest
+def meet_kernel(bit, first, p_ref, *rest):
+    if first:
+        order_hbm, pair_ref, gram_a, gram_b, old_ref, moving, order_ref, high_ref, load_sems, *rest = rest
+        low_ref = None
+    else:
+        high_ref, low_ref, moving, pair_ref, gram_a, gram_b, *rest = rest
+        old_ref = p_ref
+    part_a, landed_a, handed, part_b, landed_b, g_ref, swap_sems, sums, hands = rest
+    kind = part_b.dtype
+    kk_ref, km_ref, mm_ref = g_ref.at[0], g_ref.at[1], g_ref.at[2]
     group = lax.axis_size("rows")
     ring = group // 2
     me_r, me_c = lax.axis_index("rows"), lax.axis_index("cols")
@@ -98,7 +105,6 @@
     rows_each = quarter // group
     partner = me_c + (1 << bit) * (1 - 2 * ((me_c // (1 << bit)) % 2))
     sems_a, sems_b = sums.at[0], sums.at[1]
-    kk_ref, km_ref, mm_ref = g_ref.at[0], g_ref.at[1], g_ref.at[2]
 
     def each_peer(act):
         def visit(i, carry):
@@ -125,7 +131,7 @@
     def swap(t):
         return to(
             (me_r, partner),
-            new_ref.at[rows_of(t), :],
+            moving.at[rows_of(t), :],
             pair_ref.at[rows_of(t), half:],
             swap_sems.at[0, t],
             swap_sems.at[1, t],
@@ -157,6 +163,17 @@
             ).start()
         )
 
+    def with_low_diagonals(block):
+        high, low = split(block)
+        row = lax.broadcasted_iota(jnp.int32, block.shape, 0) % rows_each + me_r * rows_each
+        col = lax.broadcasted_iota(jnp.int32, block.shape, 1)
+        low = low.astype(F32)
+        first_low = jnp.sum(jnp.where(col == row, low, 0.0), axis=1, keepdims=True)
+        last_low = jnp.sum(jnp.where(col == row + half, low, 0.0), axis=1, keepdims=True)
+        lane = lax.broadcasted_iota(jnp.int32, (block.shape[0], quarter), 1)
+        lows = jnp.where(lane == 0, first_low, jnp.where(lane == 1, last_low, 0.0))
+        return jnp.concatenate([high, lows.astype(BF)], axis=1)
+
     barrier = pltpu.get_barrier_semaphore()
     each_peer(
         lambda peer: pl.semaphore_signal(
@@ -166,10 +183,25 @@
     pl.semaphore_signal(barrier, inc=1, device_id=(me_r, partner), device_id_type=MESH)
 
     g_ref[...] = jnp.zeros_like(g_ref)
+    if first:
+        load = pltpu.make_async_copy(p_ref, old_ref, load_sems.at[0])
+        load.start()
+        load_order = pltpu.make_async_copy(order_hbm, order_ref, load_sems.at[1])
+        load_order.start()
+        load_order.wait()
+        old_place = lax.broadcasted_iota(jnp.int32, (total, total), 0)
+        high_ref[...] = jnp.where(old_place == order_ref[...], 1.0, 0.0).astype(BF)
+        load.wait()
+
+        def order_moving(t, carry):
+            moving[rows_of(t), :] = dot(old_ref[rows_of(t), :], high_ref[:, half:]).astype(BF)
+            return carry
+
+        lax.fori_loop(0, tiles, order_moving, 0)
 
     def turn_kept(t, carry):
-        old = p_ref[rows_of(t), :]
-        new = dot(old, high_ref[...])
+        old = old_ref[rows_of(t), :]
+        new = dot(old, high_ref[:, :half])
         if low_ref is not None:
             new += dot(old, low_ref[...])
         new = new.astype(BF)
@@ -177,48 +209,50 @@
         kk_ref[...] += dot_tn(new, new)
         return carry
 
-    lax.fori_loop(0, tiles, turn_kept, 0)
-    pl.semaphore_wait(barrier, group)
+    def square_moving(t, carry):
+        block = moving[rows_of(t), :]
+        mm_ref[...] += dot_tn(block, block)
+        return carry
 
     def leave(t, carry):
         swap(t).start()
         return carry
 
+    lax.fori_loop(0, tiles, turn_kept, 0)
+    if not first:
+        lax.fori_loop(0, tiles, square_moving, 0)
+    pl.semaphore_wait(barrier, group)
     lax.fori_loop(0, tiles, leave, 0)
-
-    def square(t, carry):
-        old = new_ref[rows_of(t), :]
-        mm_ref[...] += dot_tn(old, old)
-        return carry
-
-    lax.fori_loop(0, tiles, square, 0)
+    if first:
+        lax.fori_loop(0, tiles, square_moving, 0)
     shape = (group, rows_each, half + quarter)
     part_a[...] = jnp.concatenate(
         [packed(kk_ref[...]).reshape(shape), packed(mm_ref[...]).reshape(shape)], axis=1
-    ).astype(kind)
+    ).astype(BF)
     start_sum(part_a, landed_a, sems_a)
 
+    hand = to((me_r, partner), gram_a.at[me_r], handed, hands.at[0], hands.at[1])
+
+    def reduce_a():
+        gram_a[me_r] = with_low_diagonals(end_sum(landed_a, sems_a))
+        hand.start()
+
     def cross(t, carry):
+        if bit:
+            pl.when(t == tiles - 1)(reduce_a)
         swap(t).wait()
         km_ref[...] += dot_tn(pair_ref[rows_of(t), :half], pair_ref[rows_of(t), half:])
         return carry
 
-    lax.fori_loop(0, tiles - 1, cross, 0)
-    if bit == 0:
-        lax.fori_loop(tiles - 1, tiles, cross, 0)
-        part_b[...] = km_ref[...].reshape(group, half // group, half).astype(kind)
-        start_sum(part_b, landed_b, sems_b)
-    mine = end_sum(landed_a, sems_a)
-    gram_a[me_r] = mine.astype(kind)
-    hand = to((me_r, partner), gram_a.at[me_r], handed, hands.at[0], hands.at[1])
-    hand.start()
-    if bit:
-        lax.fori_loop(tiles - 1, tiles, cross, 0)
-        part_b[...] = km_ref[...].reshape(group, half // group, half).astype(kind)
-        start_sum(part_b, landed_b, sems_b)
+    lax.fori_loop(0, tiles, cross, 0)
+    part_b[...] = km_ref[...].reshape(group, half // group, half).astype(kind)
+    start_sum(part_b, landed_b, sems_b)
+    if not bit:
+        reduce_a()
     hand.wait()
-    place = lax.broadcasted_iota(jnp.int32, mine.shape, 0)
-    gram_a[me_r] = jnp.where(place < rows_each, mine, handed[...].astype(F32)).astype(kind)
+    own = gram_a[me_r].astype(F32)
+    place = lax.broadcasted_iota(jnp.int32, own.shape, 0)
+    gram_a[me_r] = jnp.where(place < rows_each, own, handed[...].astype(F32)).astype(BF)
     start_gather(gram_a, sems_a)
     gram_b[me_r] = end_sum(landed_b, sems_b).astype(kind)
     start_gather(gram_b, sems_b)
@@ -230,63 +264,50 @@
     wait_all(gram_b, sems_b.at[2])
 
 
-def meet(p, *rest, bit, kind, site):
+def meet(p, *rest, bit, first, site):
     rows, total = p.shape
     half, quarter = total // 2, total // 4
     group = lax.axis_size("rows")
     chunk = half // group
+    kind = F32 if first else BF
     side = (group, chunk, half + quarter)
+    side_low = (group, chunk, total)
     full = (group, chunk, half)
-    vmem = pl.BlockSpec(memory_space=pltpu.VMEM)
+    place = pl.BlockSpec(memory_space=pl.ANY if first else pltpu.VMEM)
+    scratch = [
+        pltpu.VMEM(side, BF),
+        pltpu.VMEM(side, BF),
+        pltpu.VMEM(side_low[1:], BF),
+        pltpu.VMEM(full, kind),
+        pltpu.VMEM(full, kind),
+        pltpu.VMEM((3, half, half), F32),
+        pltpu.SemaphoreType.DMA((2, rows // TILE)),
+        pltpu.SemaphoreType.DMA((2, 4)),
+        pltpu.SemaphoreType.DMA((2,)),
+    ]
+    if first:
+        scratch = [
+            pltpu.VMEM((rows, total), BF),
+            pltpu.VMEM((rows, half), BF),
+            pltpu.VMEM((1, total), jnp.int32),
+            pltpu.VMEM((total, total), BF),
+            pltpu.SemaphoreType.DMA((2,)),
+        ] + scratch
     return pl.pallas_call(
-        functools.partial(meet_kernel, bit, kind),
+        functools.partial(meet_kernel, bit, first),
         out_shape=(
             jax.ShapeDtypeStruct((rows, total), BF),
-            jax.ShapeDtypeStruct(side, kind),
+            jax.ShapeDtypeStruct(side_low, BF),
             jax.ShapeDtypeStruct(full, kind),
         ),
-        in_specs=[vmem] * (1 + len(rest)),
-        out_specs=[vmem] * 3,
-        scratch_shapes=[
-            pltpu.VMEM(side, kind),
-            pltpu.VMEM(side, kind),
-            pltpu.VMEM(side[1:], kind),
-            pltpu.VMEM(full, kind),
-            pltpu.VMEM(full, kind),
-            pltpu.VMEM((3, half, half), F32),
-            pltpu.SemaphoreType.DMA((2, rows // TILE)),
-            pltpu.SemaphoreType.DMA((2, 4)),
-            pltpu.SemaphoreType.DMA((2,)),
-        ],
+        in_specs=[place] * (1 + len(rest)),
+        out_specs=[pl.BlockSpec(memory_space=pltpu.VMEM)] * 3,
+        scratch_shapes=scratch,
         compiler_params=pltpu.CompilerParams(
             collective_id=site, has_side_effects=True, vmem_limit_bytes=48 << 20
         ),
         name=f"meet_bit{bit}",
     )(p, *rest)
-
-
-def start_kernel(p_ref, order_ref, high_ref, new_ref):
-    rows, total = p_ref.shape
-    half = total // 2
-    old = lax.broadcasted_iota(jnp.int32, (total, total), 0)
-    pick = jnp.where(old == order_ref[...], 1.0, 0.0).astype(BF)
-    high_ref[...] = pick[:, :half]
-    for t in range(0, rows, TILE):
-        new_ref[t : t + TILE, :] = dot(p_ref[t : t + TILE, :], pick[:, half:]).astype(BF)
-
-
-def start(p, order):
-    rows, total = p.shape
-    half = total // 2
-    return pl.pallas_call(
-        start_kernel,
-        out_shape=(
-            jax.ShapeDtypeStruct((total, half), BF),
-            jax.ShapeDtypeStruct((rows, half), BF),
-        ),
-        compiler_params=pltpu.CompilerParams(vmem_limit_bytes=48 << 20),
-        name="start",
-    )(p, order)
 
 
 def turn_kernel(last, p_ref, gram_a, gram_b, *outs):
@@ -296,32 +317,53 @@
     group = gram_a.shape[0]
     each = quarter // group
     g = gram_a[...].astype(F32)
-    kk = unpacked(g[:, :each, :].reshape(quarter, -1))
-    mm = unpacked(g[:, each:, :].reshape(quarter, -1))
+    eye = lax.broadcasted_iota(jnp.int32, (half, half), 0) == lax.broadcasted_iota(
+        jnp.int32, (half, half), 1
+    )
+
+    def whole(part):
+        part = part.reshape(quarter, -1)
+        wide = half + quarter
+        low = jnp.concatenate([part[:, wide : wide + 1], part[:, wide + 1 : wide + 2]], axis=0)
+        return unpacked(part[:, :wide]) + jnp.where(eye, low, 0.0)
+
+    kk, mm = whole(g[:, :each, :]), whole(g[:, each:, :])
     high, low = split(rotation(kk, gram_b[...].astype(F32).reshape(half, half), mm))
     if not last:
-        high_ref, low_ref, new_ref = outs
+        high_ref, low_ref, moving = outs
         high_ref[...], low_ref[...] = high[:, :half], low[:, :half]
-        high, low = high[:, half:], low[:, half:]
-    for t in range(0, rows, TILE):
-        tile = p_ref[t : t + TILE, :]
-        out = dot(tile, high) + dot(tile, low)
-        if last:
-            outs[0][t : t + TILE, :] = out
-        else:
-            new_ref[t : t + TILE, :] = out.astype(BF)
+        for t in range(0, rows, TILE):
+            tile = p_ref[t : t + TILE, :]
+            moving[t : t + TILE, :] = (dot(tile, high[:, half:]) + dot(tile, low[:, half:])).astype(BF)
+        return
+    out_ref, tiles, sems = outs
+    copies = []
+    for t in range(rows // TILE):
+        here = pl.ds(t * TILE, TILE)
+        tile = p_ref[t * TILE : (t + 1) * TILE, :]
+        tiles[t] = dot(tile, high) + dot(tile, low)
+        copies.append(pltpu.make_async_copy(tiles.at[t], out_ref.at[here, :], sems.at[t]))
+        copies[-1].start()
+    for copy in copies:
+        copy.wait()
 
 
 def turn(p, gram_a, gram_b, last):
     rows, total = p.shape
-    half = total // 2
-    out_shape = [jax.ShapeDtypeStruct((rows, total), F32)]
-    if not last:
-        out_shape = [jax.ShapeDtypeStruct((total, half), BF)] * 2
-        out_shape += [jax.ShapeDtypeStruct((rows, half), BF)]
+    vmem = pl.BlockSpec(memory_space=pltpu.VMEM)
+    if last:
+        out = [jax.ShapeDtypeStruct((rows, total), F32)]
+        scratch = [pltpu.VMEM((rows // TILE, TILE, total), F32)]
+        scratch += [pltpu.SemaphoreType.DMA((rows // TILE,))]
+    else:
+        out = [jax.ShapeDtypeStruct((total, total // 2), BF)] * 2
+        out, scratch = out + [jax.ShapeDtypeStruct((rows, total // 2), BF)], []
     return pl.pallas_call(
         functools.partial(turn_kernel, last),
-        out_shape=out_shape,
+        out_shape=out,
+        in_specs=[vmem] * 3,
+        out_specs=[pl.BlockSpec(memory_space=pl.ANY)] if last else [vmem] * 3,
+        scratch_shapes=scratch,
         compiler_params=pltpu.CompilerParams(vmem_limit_bytes=48 << 20),
         name="last_turn" if last else "turn",
     )(p, gram_a, gram_b)
@@ -329,10 +371,10 @@
 
 def shards(columns, column_order, section_bits):
     levels = lax.axis_size("cols").bit_length() - 1
-    p, rest = columns, start(columns, column_order.reshape(1, -1))
+    p, rest = columns, [column_order.reshape(1, -1)]
     for s in range(SECTIONS):
         branches = [
-            functools.partial(meet, bit=bit, kind=BF if s else F32, site=s * levels + bit)
+            functools.partial(meet, bit=bit, first=s == 0, site=s * levels + bit)
             for bit in range(levels)
         ]
         p, gram_a, gram_b = lax.switch(section_bits[s], branches, p, *rest)

time: 121 us -> 117 us (0.967)
  Pallas kernels: 117 us -> 113 us
    pallas_call x7 -> x6, Pallas kernels: 117 us -> 113 us  [the longest x3 99.8 us: meet(): pl.pallas_call(functools.partial(meet_kernel, bit, first), out_shape=(jax...]
where the time goes in v2:
time: 117 us
  Pallas kernels  113 us (97%)
  between operations  2.12 us (2%)
  local copies, waits for them, and re-layouts  1.38 us (1%)
    pallas_call x3, Pallas kernels, meet(): pl.pallas_call(functools.partial(meet_kernel, bit, first), out_shape=(jax...  99.8 us
    pallas_call x3, Pallas kernels, turn(): pl.pallas_call(functools.partial(turn_kernel, last), out_shape=out, in_sp...  13.1 us

profile of v2, /device:TPU:8, one launch (start us, length us, event | category | flops | bytes accessed | tf_op | source)
XLA Modules:
  0.0 116.7 jit_solution(13719144014361178078)
XLA Ops:
  0.0 1.4 %fusion = (s32[1]{0:T(128)}, s32[1]{0:T(128)}, s32[1]{0:T(128)}) fusion(s32[3]{0:T(128)} %param.17), kind=kLoop, calls=%fused_computation | loop fusion | bytes 24 | tf_op jit(solution)/shard_map/slice | solution.py:380
  3.3 34.4 %conditional.3 = ((bf16[1024,512]{1,0:T(8,128)(2,1)S(1)}, bf16[16,16,512]{2,1,0:T(8,128)(2,1)S(1)}, f32[16,16,256]{2,1,0:T(8,128)S(1)})) conditional(s32[]{:T(128)} %bitcast.2, (bf16[1024,512]{1,0:T(8,128)(2,1)}, s32[1,512]{1,0:T(1,128)}) %tuple.70, (bf16[1024,512]{1,0:T(8,128)(2,1)}, s32[1,512]{1,0:T(1,128)}) %tuple.71, ...), branch_computations={%region_0.0_spmd, %region_1.0_spmd, %region_2.0_spmd, %region_3.0_... | conditional | bytes 8 | solution.py:380
  3.3 34.4 %meet_bit0.3 = (bf16[1024,512]{1,0:T(8,128)(2,1)S(1)}, bf16[16,16,512]{2,1,0:T(8,128)(2,1)S(1)}, f32[16,16,256]{2,1,0:T(8,128)S(1)}) custom-call(bf16[1024,512]{1,0:T(8,128)(2,1)} %get-tuple-element.85.p_ref, s32[1,512]{1,0:T(1,128)} %get-tuple-element.86.rest_0_), custom_call_target="tpu_custom_call" | custom-call | tf_op jit(solution)/shard_map/cond/branch_0_fun/meet_bit0/pallas_call | solution.py:296
  37.7 3.9 %turn.2 = (bf16[512,256]{1,0:T(8,128)(2,1)S(1)}, bf16[512,256]{1,0:T(8,128)(2,1)S(1)}, bf16[1024,256]{1,0:T(8,128)(2,1)S(1)}) custom-call(bf16[1024,512]{1,0:T(8,128)(2,1)S(1)} %get-tuple-element.140.p_ref, bf16[16,16,512]{2,1,0:T(8,128)(2,1)S(1)} %get-tuple-element.141.gram_a, f32[16,16,256]{2,1,0:T(8,128)S(1)} %get-tuple-element.142.gram_b), custom_call_target="tpu_custom_call" | custom-call | tf_op jit(solution)/shard_map/turn/pallas_call | solution.py:361
  41.6 34.0 %conditional.4 = ((bf16[1024,512]{1,0:T(8,128)(2,1)S(1)}, bf16[16,16,512]{2,1,0:T(8,128)(2,1)S(1)}, bf16[16,16,256]{2,1,0:T(8,128)(2,1)S(1)})) conditional(s32[]{:T(128)} %bitcast.1, (bf16[1024,512]{1,0:T(8,128)(2,1)S(1)}, bf16[512,256]{1,0:T(8,128)(2,1)S(1)}, bf16[512,256]{1,0:T(8,128)(2,1)S(1)}, ...), branch_computations={%region_4.0_spmd, %region_5.0_spmd, %region_6.0_spmd, %region_7.0_... | conditional | bytes 8 | solution.py:380
  41.7 33.7 %meet_bit3.4 = (bf16[1024,512]{1,0:T(8,128)(2,1)S(1)}, bf16[16,16,512]{2,1,0:T(8,128)(2,1)S(1)}, bf16[16,16,256]{2,1,0:T(8,128)(2,1)S(1)}) custom-call(bf16[1024,512]{1,0:T(8,128)(2,1)S(1)} %get-tuple-element.105.p_ref, bf16[512,256]{1,0:T(8,128)(2,1)S(1)} %get-tuple-element.106.rest_0_, bf16[512,256]{1,0:T(8,128)(2,1)S(1)} %get-tuple-element.107.rest_1_, ...), custom_call_target="tpu_custom_call" | custom-call | tf_op jit(solution)/shard_map/cond/branch_3_fun/meet_bit3/pallas_call | solution.py:296
  75.6 3.9 %turn.3 = (bf16[512,256]{1,0:T(8,128)(2,1)S(1)}, bf16[512,256]{1,0:T(8,128)(2,1)S(1)}, bf16[1024,256]{1,0:T(8,128)(2,1)S(1)}) custom-call(bf16[1024,512]{1,0:T(8,128)(2,1)S(1)} %get-tuple-element.146.p_ref, bf16[16,16,512]{2,1,0:T(8,128)(2,1)S(1)} %get-tuple-element.147.gram_a, bf16[16,16,256]{2,1,0:T(8,128)(2,1)S(1)} %get-tuple-element.148.gram_b), custom_call_target="tpu_custom_call" | custom-call | tf_op jit(solution)/shard_map/turn/pallas_call | solution.py:361
  79.5 31.7 %conditional.5 = ((bf16[1024,512]{1,0:T(8,128)(2,1)S(1)}, bf16[16,16,512]{2,1,0:T(8,128)(2,1)S(1)}, bf16[16,16,256]{2,1,0:T(8,128)(2,1)S(1)})) conditional(s32[]{:T(128)} %bitcast, (bf16[1024,512]{1,0:T(8,128)(2,1)S(1)}, bf16[512,256]{1,0:T(8,128)(2,1)S(1)}, bf16[512,256]{1,0:T(8,128)(2,1)S(1)}, ...), branch_computations={%region_8.0_spmd, %region_9.0_spmd, %region_10.0_spmd, %region_11.... | conditional | bytes 8 | solution.py:380
  79.5 31.7 %meet_bit3.5 = (bf16[1024,512]{1,0:T(8,128)(2,1)S(1)}, bf16[16,16,512]{2,1,0:T(8,128)(2,1)S(1)}, bf16[16,16,256]{2,1,0:T(8,128)(2,1)S(1)}) custom-call(bf16[1024,512]{1,0:T(8,128)(2,1)S(1)} %get-tuple-element.121.p_ref, bf16[512,256]{1,0:T(8,128)(2,1)S(1)} %get-tuple-element.122.rest_0_, bf16[512,256]{1,0:T(8,128)(2,1)S(1)} %get-tuple-element.123.rest_1_, ...), custom_call_target="tpu_custom_call" | custom-call | tf_op jit(solution)/shard_map/cond/branch_3_fun/meet_bit3/pallas_call | solution.py:296
  111.2 5.3 %last_turn.1 = f32[1024,512]{1,0:T(8,128)} custom-call(bf16[1024,512]{1,0:T(8,128)(2,1)S(1)} %get-tuple-element.152.p_ref, bf16[16,16,512]{2,1,0:T(8,128)(2,1)S(1)} %get-tuple-element.153.gram_a, bf16[16,16,256]{2,1,0:T(8,128)(2,1)S(1)} %get-tuple-element.154.gram_b), custom_call_target="tpu_custom_call" | custom-call | tf_op jit(solution)/shard_map/last_turn/pallas_call | solution.py:361

commit v3 on v2

--- a/solution.py
+++ b/solution.py
@@ -182,7 +182,6 @@
     )
     pl.semaphore_signal(barrier, inc=1, device_id=(me_r, partner), device_id_type=MESH)
 
-    g_ref[...] = jnp.zeros_like(g_ref)
     if first:
         load = pltpu.make_async_copy(p_ref, old_ref, load_sems.at[0])
         load.start()
@@ -204,27 +203,34 @@
         new = dot(old, high_ref[:, :half])
         if low_ref is not None:
             new += dot(old, low_ref[...])
-        new = new.astype(BF)
-        pair_ref[rows_of(t), :half] = new
-        kk_ref[...] += dot_tn(new, new)
+        pair_ref[rows_of(t), :half] = new.astype(BF)
         return carry
 
-    def square_moving(t, carry):
-        block = moving[rows_of(t), :]
-        mm_ref[...] += dot_tn(block, block)
+    def square(t, carry):
+        kept, leaving = pair_ref[rows_of(t), :half], moving[rows_of(t), :]
+        kk_ref[...] += dot_tn(kept, kept)
+        mm_ref[...] += dot_tn(leaving, leaving)
         return carry
 
     def leave(t, carry):
         swap(t).start()
         return carry
 
-    lax.fori_loop(0, tiles, turn_kept, 0)
-    if not first:
-        lax.fori_loop(0, tiles, square_moving, 0)
+    def local():
+        g_ref[...] = jnp.zeros_like(g_ref)
+        lax.fori_loop(0, tiles, square, 0)
+
+    slow = bit != 0
+    if not (first and slow):
+        lax.fori_loop(0, tiles, turn_kept, 0)
+    if not slow:
+        local()
     pl.semaphore_wait(barrier, group)
     lax.fori_loop(0, tiles, leave, 0)
-    if first:
-        lax.fori_loop(0, tiles, square_moving, 0)
+    if first and slow:
+        lax.fori_loop(0, tiles, turn_kept, 0)
+    if slow:
+        local()
     shape = (group, rows_each, half + quarter)
     part_a[...] = jnp.concatenate(
         [packed(kk_ref[...]).reshape(shape), packed(mm_ref[...]).reshape(shape)], axis=1

time: 117 us -> 115 us (0.983)
  Pallas kernels: 113 us -> 110 us
    pallas_call x3, Pallas kernels: 99.8 us -> 96.9 us  [meet(): pl.pallas_call(functools.partial(meet_kernel, bit, first), out_shape=(jax...]
where the time goes in v3:
time: 115 us; the launch traced here: 114 us
  Pallas kernels  110 us (96%)
  between operations  2.12 us (2%)
  local copies, waits for them, and re-layouts  1.38 us (1%)
    pallas_call x3, Pallas kernels, meet(): pl.pallas_call(functools.partial(meet_kernel, bit, first), out_shape=(jax...  96.9 us
    pallas_call x3, Pallas kernels, turn(): pl.pallas_call(functools.partial(turn_kernel, last), out_shape=out, in_sp...  13.1 us

profile of v3, /device:TPU:8, one launch (start us, length us, event | category | flops | bytes accessed | tf_op | source)
XLA Modules:
  0.0 113.8 jit_solution(3063907113229497759)
XLA Ops:
  0.0 1.4 %fusion = (s32[1]{0:T(128)}, s32[1]{0:T(128)}, s32[1]{0:T(128)}) fusion(s32[3]{0:T(128)} %param.17), kind=kLoop, calls=%fused_computation | loop fusion | bytes 24 | tf_op jit(solution)/shard_map/slice | solution.py:386
  3.3 43.0 %conditional.3 = ((bf16[1024,512]{1,0:T(8,128)(2,1)S(1)}, bf16[16,16,512]{2,1,0:T(8,128)(2,1)S(1)}, f32[16,16,256]{2,1,0:T(8,128)S(1)})) conditional(s32[]{:T(128)} %bitcast.2, (bf16[1024,512]{1,0:T(8,128)(2,1)}, s32[1,512]{1,0:T(1,128)}) %tuple.70, (bf16[1024,512]{1,0:T(8,128)(2,1)}, s32[1,512]{1,0:T(1,128)}) %tuple.71, ...), branch_computations={%region_0.0_spmd, %region_1.0_spmd, %region_2.0_spmd, %region_3.0_... | conditional | bytes 8 | solution.py:386
  3.3 43.0 %meet_bit3.3 = (bf16[1024,512]{1,0:T(8,128)(2,1)S(1)}, bf16[16,16,512]{2,1,0:T(8,128)(2,1)S(1)}, f32[16,16,256]{2,1,0:T(8,128)S(1)}) custom-call(bf16[1024,512]{1,0:T(8,128)(2,1)} %get-tuple-element.91.p_ref, s32[1,512]{1,0:T(1,128)} %get-tuple-element.92.rest_0_), custom_call_target="tpu_custom_call" | custom-call | tf_op jit(solution)/shard_map/cond/branch_3_fun/meet_bit3/pallas_call | solution.py:302
  46.3 3.9 %turn.2 = (bf16[512,256]{1,0:T(8,128)(2,1)S(1)}, bf16[512,256]{1,0:T(8,128)(2,1)S(1)}, bf16[1024,256]{1,0:T(8,128)(2,1)S(1)}) custom-call(bf16[1024,512]{1,0:T(8,128)(2,1)S(1)} %get-tuple-element.140.p_ref, bf16[16,16,512]{2,1,0:T(8,128)(2,1)S(1)} %get-tuple-element.141.gram_a, f32[16,16,256]{2,1,0:T(8,128)S(1)} %get-tuple-element.142.gram_b), custom_call_target="tpu_custom_call" | custom-call | tf_op jit(solution)/shard_map/turn/pallas_call | solution.py:367
  50.2 31.5 %conditional.4 = ((bf16[1024,512]{1,0:T(8,128)(2,1)S(1)}, bf16[16,16,512]{2,1,0:T(8,128)(2,1)S(1)}, bf16[16,16,256]{2,1,0:T(8,128)(2,1)S(1)})) conditional(s32[]{:T(128)} %bitcast.1, (bf16[1024,512]{1,0:T(8,128)(2,1)S(1)}, bf16[512,256]{1,0:T(8,128)(2,1)S(1)}, bf16[512,256]{1,0:T(8,128)(2,1)S(1)}, ...), branch_computations={%region_4.0_spmd, %region_5.0_spmd, %region_6.0_spmd, %region_7.0_... | conditional | bytes 8 | solution.py:386
  50.3 31.3 %meet_bit3.4 = (bf16[1024,512]{1,0:T(8,128)(2,1)S(1)}, bf16[16,16,512]{2,1,0:T(8,128)(2,1)S(1)}, bf16[16,16,256]{2,1,0:T(8,128)(2,1)S(1)}) custom-call(bf16[1024,512]{1,0:T(8,128)(2,1)S(1)} %get-tuple-element.105.p_ref, bf16[512,256]{1,0:T(8,128)(2,1)S(1)} %get-tuple-element.106.rest_0_, bf16[512,256]{1,0:T(8,128)(2,1)S(1)} %get-tuple-element.107.rest_1_, ...), custom_call_target="tpu_custom_call" | custom-call | tf_op jit(solution)/shard_map/cond/branch_3_fun/meet_bit3/pallas_call | solution.py:302
  81.8 3.9 %turn.3 = (bf16[512,256]{1,0:T(8,128)(2,1)S(1)}, bf16[512,256]{1,0:T(8,128)(2,1)S(1)}, bf16[1024,256]{1,0:T(8,128)(2,1)S(1)}) custom-call(bf16[1024,512]{1,0:T(8,128)(2,1)S(1)} %get-tuple-element.146.p_ref, bf16[16,16,512]{2,1,0:T(8,128)(2,1)S(1)} %get-tuple-element.147.gram_a, bf16[16,16,256]{2,1,0:T(8,128)(2,1)S(1)} %get-tuple-element.148.gram_b), custom_call_target="tpu_custom_call" | custom-call | tf_op jit(solution)/shard_map/turn/pallas_call | solution.py:367
  85.7 22.7 %conditional.5 = ((bf16[1024,512]{1,0:T(8,128)(2,1)S(1)}, bf16[16,16,512]{2,1,0:T(8,128)(2,1)S(1)}, bf16[16,16,256]{2,1,0:T(8,128)(2,1)S(1)})) conditional(s32[]{:T(128)} %bitcast, (bf16[1024,512]{1,0:T(8,128)(2,1)S(1)}, bf16[512,256]{1,0:T(8,128)(2,1)S(1)}, bf16[512,256]{1,0:T(8,128)(2,1)S(1)}, ...), branch_computations={%region_8.0_spmd, %region_9.0_spmd, %region_10.0_spmd, %region_11.... | conditional | bytes 8 | solution.py:386
  85.7 22.6 %meet_bit0.5 = (bf16[1024,512]{1,0:T(8,128)(2,1)S(1)}, bf16[16,16,512]{2,1,0:T(8,128)(2,1)S(1)}, bf16[16,16,256]{2,1,0:T(8,128)(2,1)S(1)}) custom-call(bf16[1024,512]{1,0:T(8,128)(2,1)S(1)} %get-tuple-element.109.p_ref, bf16[512,256]{1,0:T(8,128)(2,1)S(1)} %get-tuple-element.110.rest_0_, bf16[512,256]{1,0:T(8,128)(2,1)S(1)} %get-tuple-element.111.rest_1_, ...), custom_call_target="tpu_custom_call" | custom-call | tf_op jit(solution)/shard_map/cond/branch_0_fun/meet_bit0/pallas_call | solution.py:302
  108.3 5.3 %last_turn.1 = f32[1024,512]{1,0:T(8,128)} custom-call(bf16[1024,512]{1,0:T(8,128)(2,1)S(1)} %get-tuple-element.152.p_ref, bf16[16,16,512]{2,1,0:T(8,128)(2,1)S(1)} %get-tuple-element.153.gram_a, bf16[16,16,256]{2,1,0:T(8,128)(2,1)S(1)} %get-tuple-element.154.gram_b), custom_call_target="tpu_custom_call" | custom-call | tf_op jit(solution)/shard_map/last_turn/pallas_call | solution.py:367

commit v4 on v3

--- a/solution.py
+++ b/solution.py
@@ -74,7 +74,7 @@
         zb = z.astype(BF)
         w = dot_nt(zb, zb)
         if k:
-            w = w + (z + z.T)
+            w = w + (z + zb.T.astype(F32))
         square = scale * scale
         b = 1.5 - 0.5 * square
         z = z - (0.5 * square / b) * (w + dot(zb, w.astype(BF)))

time: 115 us -> 112 us (0.974)
  Pallas kernels: 110 us -> 106 us
    pallas_call x3, Pallas kernels: 96.9 us -> 93.4 us  [meet(): pl.pallas_call(functools.partial(meet_kernel, bit, first), out_shape=(jax...]
where the time goes in v4:
time: 112 us; the launch traced here: 110 us
  Pallas kernels  106 us (95%)
  between operations  2.12 us (2%)
  local copies, waits for them, and re-layouts  1.38 us (1%)
    pallas_call x3, Pallas kernels, meet(): pl.pallas_call(functools.partial(meet_kernel, bit, first), out_shape=(jax...  93.4 us
    pallas_call x3, Pallas kernels, turn(): pl.pallas_call(functools.partial(turn_kernel, last), out_shape=out, in_sp...  13 us

profile of v4, /device:TPU:8, one launch (start us, length us, event | category | flops | bytes accessed | tf_op | source)
XLA Modules:
  0.0 110.2 jit_solution(8984630833465868973)
XLA Ops:
  0.0 1.4 %fusion = (s32[1]{0:T(128)}, s32[1]{0:T(128)}, s32[1]{0:T(128)}) fusion(s32[3]{0:T(128)} %param.17), kind=kLoop, calls=%fused_computation | loop fusion | bytes 24 | tf_op jit(solution)/shard_map/slice | solution.py:386
  3.3 33.6 %conditional.3 = ((bf16[1024,512]{1,0:T(8,128)(2,1)S(1)}, bf16[16,16,512]{2,1,0:T(8,128)(2,1)S(1)}, f32[16,16,256]{2,1,0:T(8,128)S(1)})) conditional(s32[]{:T(128)} %bitcast.2, (bf16[1024,512]{1,0:T(8,128)(2,1)}, s32[1,512]{1,0:T(1,128)}) %tuple.70, (bf16[1024,512]{1,0:T(8,128)(2,1)}, s32[1,512]{1,0:T(1,128)}) %tuple.71, ...), branch_computations={%region_0.0_spmd, %region_1.0_spmd, %region_2.0_spmd, %region_3.0_... | conditional | bytes 8 | solution.py:386
  3.3 33.6 %meet_bit0.3 = (bf16[1024,512]{1,0:T(8,128)(2,1)S(1)}, bf16[16,16,512]{2,1,0:T(8,128)(2,1)S(1)}, f32[16,16,256]{2,1,0:T(8,128)S(1)}) custom-call(bf16[1024,512]{1,0:T(8,128)(2,1)} %get-tuple-element.85.p_ref, s32[1,512]{1,0:T(1,128)} %get-tuple-element.86.rest_0_), custom_call_target="tpu_custom_call" | custom-call | tf_op jit(solution)/shard_map/cond/branch_0_fun/meet_bit0/pallas_call | solution.py:302
  36.9 3.9 %turn.2 = (bf16[512,256]{1,0:T(8,128)(2,1)S(1)}, bf16[512,256]{1,0:T(8,128)(2,1)S(1)}, bf16[1024,256]{1,0:T(8,128)(2,1)S(1)}) custom-call(bf16[1024,512]{1,0:T(8,128)(2,1)S(1)} %get-tuple-element.140.p_ref, bf16[16,16,512]{2,1,0:T(8,128)(2,1)S(1)} %get-tuple-element.141.gram_a, f32[16,16,256]{2,1,0:T(8,128)S(1)} %get-tuple-element.142.gram_b), custom_call_target="tpu_custom_call" | custom-call | tf_op jit(solution)/shard_map/turn/pallas_call | solution.py:367
  40.8 32.7 %conditional.4 = ((bf16[1024,512]{1,0:T(8,128)(2,1)S(1)}, bf16[16,16,512]{2,1,0:T(8,128)(2,1)S(1)}, bf16[16,16,256]{2,1,0:T(8,128)(2,1)S(1)})) conditional(s32[]{:T(128)} %bitcast.1, (bf16[1024,512]{1,0:T(8,128)(2,1)S(1)}, bf16[512,256]{1,0:T(8,128)(2,1)S(1)}, bf16[512,256]{1,0:T(8,128)(2,1)S(1)}, ...), branch_computations={%region_4.0_spmd, %region_5.0_spmd, %region_6.0_spmd, %region_7.0_... | conditional | bytes 8 | solution.py:386
  40.8 32.5 %meet_bit3.4 = (bf16[1024,512]{1,0:T(8,128)(2,1)S(1)}, bf16[16,16,512]{2,1,0:T(8,128)(2,1)S(1)}, bf16[16,16,256]{2,1,0:T(8,128)(2,1)S(1)}) custom-call(bf16[1024,512]{1,0:T(8,128)(2,1)S(1)} %get-tuple-element.105.p_ref, bf16[512,256]{1,0:T(8,128)(2,1)S(1)} %get-tuple-element.106.rest_0_, bf16[512,256]{1,0:T(8,128)(2,1)S(1)} %get-tuple-element.107.rest_1_, ...), custom_call_target="tpu_custom_call" | custom-call | tf_op jit(solution)/shard_map/cond/branch_3_fun/meet_bit3/pallas_call | solution.py:302
  73.5 3.9 %turn.3 = (bf16[512,256]{1,0:T(8,128)(2,1)S(1)}, bf16[512,256]{1,0:T(8,128)(2,1)S(1)}, bf16[1024,256]{1,0:T(8,128)(2,1)S(1)}) custom-call(bf16[1024,512]{1,0:T(8,128)(2,1)S(1)} %get-tuple-element.146.p_ref, bf16[16,16,512]{2,1,0:T(8,128)(2,1)S(1)} %get-tuple-element.147.gram_a, bf16[16,16,256]{2,1,0:T(8,128)(2,1)S(1)} %get-tuple-element.148.gram_b), custom_call_target="tpu_custom_call" | custom-call | tf_op jit(solution)/shard_map/turn/pallas_call | solution.py:367
  77.4 27.3 %conditional.5 = ((bf16[1024,512]{1,0:T(8,128)(2,1)S(1)}, bf16[16,16,512]{2,1,0:T(8,128)(2,1)S(1)}, bf16[16,16,256]{2,1,0:T(8,128)(2,1)S(1)})) conditional(s32[]{:T(128)} %bitcast, (bf16[1024,512]{1,0:T(8,128)(2,1)S(1)}, bf16[512,256]{1,0:T(8,128)(2,1)S(1)}, bf16[512,256]{1,0:T(8,128)(2,1)S(1)}, ...), branch_computations={%region_8.0_spmd, %region_9.0_spmd, %region_10.0_spmd, %region_11.... | conditional | bytes 8 | solution.py:386
  77.5 27.3 %meet_bit1.5 = (bf16[1024,512]{1,0:T(8,128)(2,1)S(1)}, bf16[16,16,512]{2,1,0:T(8,128)(2,1)S(1)}, bf16[16,16,256]{2,1,0:T(8,128)(2,1)S(1)}) custom-call(bf16[1024,512]{1,0:T(8,128)(2,1)S(1)} %get-tuple-element.113.p_ref, bf16[512,256]{1,0:T(8,128)(2,1)S(1)} %get-tuple-element.114.rest_0_, bf16[512,256]{1,0:T(8,128)(2,1)S(1)} %get-tuple-element.115.rest_1_, ...), custom_call_target="tpu_custom_call" | custom-call | tf_op jit(solution)/shard_map/cond/branch_1_fun/meet_bit1/pallas_call | solution.py:302
  104.8 5.3 %last_turn.1 = f32[1024,512]{1,0:T(8,128)} custom-call(bf16[1024,512]{1,0:T(8,128)(2,1)S(1)} %get-tuple-element.152.p_ref, bf16[16,16,512]{2,1,0:T(8,128)(2,1)S(1)} %get-tuple-element.153.gram_a, bf16[16,16,256]{2,1,0:T(8,128)(2,1)S(1)} %get-tuple-element.154.gram_b), custom_call_target="tpu_custom_call" | custom-call | tf_op jit(solution)/shard_map/last_turn/pallas_call | solution.py:367
